TPU v7x, 128 devices: a whole 4x4x4 slice. The times are simulated.
128 devices in a mesh: group: 4 (over z), member: 32 (over y, x, core).
Axes of the slice: x: 4, y: 4, z: 4, core: 2. Of those that a mesh axis runs over, the one named last changes fastest.
Arguments:
- history: bfloat16 [65536, 64, 128], P(('group', 'member')), may hold values from -6 to 6
- near_time: bfloat16 [8, 64], replicated, may hold values from -0.75 to 0.75
- near_kernel: bfloat16 [8, 128, 128], replicated, may hold values from -0.1875 to 0.1875
- projection: bfloat16 [64, 128, 256], replicated, may hold values from -0.0625 to 0.0625
- receive_map: bfloat16 [256, 128], replicated, may hold values from -0.375 to 0.375
- self_inverse: bfloat16 [128, 128], replicated, may hold values from -0.5 to 0.5
- incident: float32 [2, 65536, 128], P(None, ('group', 'member')), may hold values from -6 to 6
- neighbours: int32 [65536, 8], P(('group', 'member')), may hold values from 0 to 65535, as said below
- send_sources: int32 [128, 128, 2], P(('group', 'member')), may hold values from -1 to 511, as said below
- recv_observers: int32 [128, 128, 2], P(('group', 'member')), may hold values from -1 to 511, as said below
- transfer: bfloat16 [128, 128, 2, 256], P(('group', 'member')), may hold values from -6 to 6
Outputs:
- currents: float32 [2, 65536, 128], P(None, ('group', 'member'))
Inputs may be any that keep to these rules, and one draw needn't show every extreme that they name: `neighbours`: every neighbour lies in the cluster's own group of 16384 consecutive clusters, at most 32 clusters from the cluster; the first slot lies 32 clusters away unless the group ends first. `send_sources`: entry [a, b, s] is a cluster of device a, numbered 0 to 511, whose rays device b needs in slot s, or -1 for an empty slot; used slots come first; devices of one group send each other nothing; some pair of devices fills all 2 slots. `recv_observers`: entry [b, a, s] is a cluster of device b, numbered 0 to 511, observing what device a sends in slot s; it is -1 exactly where send_sources[a, b, s] is -1.
All inputs are finite; a program needn't handle non-finite values.
Results may differ from a plain program's by a relative error of at most 0.0038.
Values may be sent and summed in bfloat16 or wider, within the bound.
A program may use at most 64 MiB of HBM per device.

v0:
```python
import jax
import jax.numpy as jnp
from jax import lax
from jax.sharding import PartitionSpec as P


def padded(block, sides, width):
    for axis, dim in sides:
        count = lax.axis_size(axis)
        forward = [(i, i + 1) for i in range(count - 1)]
        backward = [(target, source) for source, target in forward]
        low = lax.ppermute(
            lax.slice_in_dim(block, block.shape[dim] - width, None, axis=dim), axis, forward
        )
        high = lax.ppermute(lax.slice_in_dim(block, 0, width, axis=dim), axis, backward)
        block = jnp.concatenate([low, block, high], axis=dim)
    return block


def body(
    history,
    near_time,
    near_kernel,
    projection,
    receive_map,
    self_inverse,
    incident,
    neighbours,
    send_sources,
    recv_observers,
    transfer,
):
    cluster_count = history.shape[0]
    history_depth = history.shape[1]
    basis_width = history.shape[2]
    slot_count = near_time.shape[0]
    ray_count = projection.shape[2]
    rim_width = cluster_count // 16
    first_cluster = lax.axis_index(("group", "member")) * cluster_count - rim_width
    local_neighbours = neighbours - first_cluster
    slot_ids = jnp.arange(slot_count, dtype=jnp.int32)
    kernel_flat = near_kernel.reshape(slot_count * basis_width, basis_width)
    projection_flat = projection.reshape(history_depth * basis_width, ray_count)
    sources = send_sources[0]
    occupied = sources >= 0
    clamped = jnp.maximum(sources, 0)
    observers = recv_observers[0].reshape(-1)
    observer_table = (
        observers[None, :] == jnp.arange(cluster_count, dtype=jnp.int32)[:, None]
    ).astype(jnp.float32)
    transfer_wide = transfer[0].astype(jnp.float32)
    results = []
    for time_step in range(incident.shape[0]):
        extended = padded(history, (("member", 0),), rim_width)
        reduced = jnp.einsum(
            "jh,shb->sjb", near_time, extended, preferred_element_type=jnp.float32
        ).astype(jnp.bfloat16)
        picked = reduced[local_neighbours, slot_ids[None, :], :]
        near_field = jnp.dot(
            picked.reshape(cluster_count, slot_count * basis_width),
            kernel_flat,
            preferred_element_type=jnp.float32,
        )
        outgoing = jnp.dot(
            history.reshape(cluster_count, history_depth * basis_width),
            projection_flat,
            preferred_element_type=jnp.float32,
        ).astype(jnp.bfloat16)
        outbound = jnp.where(occupied[:, :, None], outgoing[clamped], jnp.zeros((), jnp.bfloat16))
        inbound = lax.all_to_all(
            outbound, ("group", "member"), split_axis=0, concat_axis=0, tiled=True
        )
        contributions = (transfer_wide * inbound.astype(jnp.float32)).reshape(-1, ray_count)
        incoming = jnp.dot(observer_table, contributions, precision=lax.Precision.HIGHEST).astype(
            jnp.bfloat16
        )
        far_field = jnp.dot(incoming, receive_map, preferred_element_type=jnp.float32)
        right_side = (incident[time_step] - near_field - far_field).astype(jnp.bfloat16)
        current = jnp.dot(right_side, self_inverse, preferred_element_type=jnp.float32)
        results.append(current)
        history = jnp.concatenate(
            [current.astype(jnp.bfloat16)[:, None], history[:, : history_depth - 1]], axis=1
        )
    return jnp.stack(results)


def solution(mesh):
    in_specs = (
        P(("group", "member"), None, None),
        P(),
        P(),
        P(),
        P(),
        P(),
        P(None, ("group", "member"), None),
        P(("group", "member"), None),
        P(("group", "member"), None, None),
        P(("group", "member"), None, None),
        P(("group", "member"), None, None, None),
    )
    out_specs = P(None, ("group", "member"), None)
    return jax.shard_map(body, mesh=mesh, in_specs=in_specs, out_specs=out_specs, check_vma=False)
```

profile of v0, /device:TPU:1, one launch (start us, length us, event | category | flops | bytes accessed | tf_op | source)
XLA Modules:
  0.0 148.9 jit_solution(13443939523162140591)
XLA Ops:
  0.0 0.0 copy-start
  0.0 0.7 compare_bitcast_fusion
  0.7 0.7 broadcast_maximum_fusion
  1.4 0.1 copy.18
  1.6 0.1 copy.20
  1.7 0.1 reshape.48
  1.8 0.0 copy-start.4
  1.8 0.0 copy-start.5
  1.8 0.0 copy-start.1
  1.9 0.0 copy-start.6
  1.9 9.3 %fusion.39 = bf16[512,256]{1,0:T(8,128)(2,1)S(1)} fusion(bf16[64,128,256]{2,1,0:T(8,128)(2,1)} %param.14, bf16[512,64,128]{2,1,0:T(8,128)(2,1)} %param.11), kind=kOutput, calls=%fused_computation.36 | convolution fusion | flops 2147614720 | bytes 12845056 | tf_op jit(solution)/shard_map/dot_general | solution.py:64
  11.2 1.2 gather_fusion.1
  12.4 0.1 reshape.47
  12.4 0.9 broadcast_select_fusion.1
  13.3 11.5 %all-to-all-start = ((bf16[128,2,256]{2,1,0:T(2,128)(2,1)}), bf16[128,2,256]{2,1,0:T(2,128)(2,1)S(1)}, u32[]{:S(2)}, u32[]{:S(2)}) async-start(bf16[128,2,256]{2,1,0:T(2,128)(2,1)} %broadcast_select_fusion.1), calls=%async_computation | async-start | bytes 262144 | tf_op jit(solution)/shard_map/all_to_all | solution.py:70
  24.8 1.3 fusion.61
  26.1 3.5 %collective-permute-start = (bf16[32,64,128]{2,1,0:T(8,128)(2,1)S(1)}, bf16[32,64,128]{2,1,0:T(8,128)(2,1)S(1)}, u32[]{:S(2)}, u32[]{:S(2)}) collective-permute-start(bf16[32,64,128]{2,1,0:T(8,128)(2,1)S(1)} %get-tuple-element.7), channel_id=1, source_target_pairs={{0,1},{1,2},{2,3},{3,4},{4,5},{5,6},{6,7},{7,8},{8,9},{9,10},{10,1... | collective-permute-start | bytes 1572872 | tf_op jit(solution)/shard_map/ppermute | solution.py:12
  29.6 1.9 %collective-permute-start.1 = (bf16[32,64,128]{2,1,0:T(8,128)(2,1)S(1)}, bf16[32,64,128]{2,1,0:T(8,128)(2,1)S(1)}, u32[]{:S(2)}, u32[]{:S(2)}) collective-permute-start(bf16[32,64,128]{2,1,0:T(8,128)(2,1)S(1)} %get-tuple-element.8), channel_id=1, source_target_pairs={{1,0},{2,1},{3,2},{4,3},{5,4},{6,5},{7,6},{8,7},{9,8},{10,9},{11,1... | collective-permute-start | bytes 1572872 | tf_op jit(solution)/shard_map/ppermute | solution.py:15
  31.6 0.0 copy-done.4
  31.6 0.0 copy-done.5
  31.6 0.1 copy.17
  31.7 0.1 eq.15
  31.9 0.1 copy.16
  32.0 0.2 reshape.40
  32.1 2.7 %all-to-all-done = bf16[128,2,256]{2,1,0:T(2,128)(2,1)S(1)} async-done(((bf16[128,2,256]{2,1,0:T(2,128)(2,1)}), bf16[128,2,256]{2,1,0:T(2,128)(2,1)S(1)}, u32[]{:S(2)}, u32[]{:S(2)}) %all-to-all-start) | async-done | bytes 131104 | tf_op jit(solution)/shard_map/all_to_all | solution.py:70
  34.8 0.0 copy-done.1
  34.8 0.1 convert_multiply_fusion.1
  35.0 0.2 reshape.37
  35.2 0.4 convolution_convert_fusion.1
  35.6 0.1 collective-permute-done
  35.7 4.4 %collective-permute-done.1 = bf16[32,64,128]{2,1,0:T(8,128)(2,1)S(1)} collective-permute-done((bf16[32,64,128]{2,1,0:T(8,128)(2,1)S(1)}, bf16[32,64,128]{2,1,0:T(8,128)(2,1)S(1)}, u32[]{:S(2)}, u32[]{:S(2)}) %collective-permute-start.1) | collective-permute-done | bytes 524320 | tf_op jit(solution)/shard_map/ppermute | solution.py:15
  40.1 0.0 copy-done.6
  40.1 5.4 %fusion.24 = bf16[576,8,128]{2,1,0:T(8,128)(2,1)S(1)} fusion(bf16[32,64,128]{2,1,0:T(8,128)(2,1)S(1)} %collective-permute-done.1, bf16[512,64,128]{2,1,0:T(8,128)(2,1)} %param.11, bf16[32,64,128]{2,1,0:T(8,128)(2,1)S(1)} %collective-permute-done, bf16[8,64]{1,0:T(8,128)(2,1)S(1)} %copy-done.6), kind=kOutput, calls=%fused_computation.29 | convolution fusion | flops 85524480 | bytes 10617856 | tf_op jit(solution)/shard_map/jh,shb->sjb/dot_general | solution.py:55
  45.5 0.0 copy-start.2
  45.5 0.0 copy-start.3
  45.5 20.9 %gather_fusion = bf16[4096,128]{1,0:T(8,128)(2,1)S(1)} fusion(bf16[576,8,128]{2,1,0:T(8,128)(2,1)S(1)} %fusion.24, s32[4096]{0:T(1024)S(1)} %reshape.40), kind=kCustom, calls=%fused_computation | custom fusion | bytes 2129920 | tf_op jit(solution)/shard_map/gather | solution.py:58
  66.5 0.0 copy-done
  66.5 1.4 fusion.42
  67.9 0.0 copy-done.2
  67.9 0.0 copy-done.3
  67.9 0.4 fusion.46
  68.3 0.2 copy.21
  68.5 11.5 %pad_maximum_fusion = bf16[512,64,128]{2,1,0:T(8,128)(2,1)} fusion(bf16[512,1,128]{2,1,0:T(2,128)(2,1)S(1)} %copy.21, bf16[512,63,128]{2,1,0:T(8,128)(2,1)} %bitcast.61), kind=kLoop, calls=%fused_computation.6 | loop fusion | flops 16777216 | bytes 16777216 | tf_op jit(solution)/shard_map/concatenate | solution.py:81
  80.0 9.3 %fusion.36 = bf16[512,256]{1,0:T(8,128)(2,1)S(1)} fusion(bf16[64,128,256]{2,1,0:T(8,128)(2,1)} %param.14, bf16[512,64,128]{2,1,0:T(8,128)(2,1)} %pad_maximum_fusion), kind=kOutput, calls=%fused_computation.35 | convolution fusion | flops 2147614720 | bytes 12845056 | tf_op jit(solution)/shard_map/dot_general | solution.py:64
  89.3 1.2 gather_fusion.3
  90.5 0.1 reshape.61
  90.6 0.9 broadcast_select_fusion
  91.4 10.9 %all-to-all-start.1 = ((bf16[128,2,256]{2,1,0:T(2,128)(2,1)}), bf16[128,2,256]{2,1,0:T(2,128)(2,1)S(1)}, u32[]{:S(2)}, u32[]{:S(2)}) async-start(bf16[128,2,256]{2,1,0:T(2,128)(2,1)} %broadcast_select_fusion), calls=%async_computation.1 | async-start | bytes 262144 | tf_op jit(solution)/shard_map/all_to_all | solution.py:70
  102.3 1.6 %fusion.49 = (bf16[32,64,128]{2,1,0:T(8,128)(2,1)S(1)}, bf16[32,64,128]{2,1,0:T(8,128)(2,1)S(1)}) fusion(bf16[512,63,128]{2,1,0:T(8,128)(2,1)} %bitcast.62, bf16[512,1,128]{2,1,0:T(2,128)(2,1)S(1)} %copy.21), kind=kLoop, calls=%fused_computation.49 | loop fusion | flops 2097152 | bytes 9437184 | tf_op jit(solution)/shard_map/concatenate | solution.py:81
  103.9 3.5 %collective-permute-start.2 = (bf16[32,64,128]{2,1,0:T(8,128)(2,1)S(1)}, bf16[32,64,128]{2,1,0:T(8,128)(2,1)}, u32[]{:S(2)}, u32[]{:S(2)}) collective-permute-start(bf16[32,64,128]{2,1,0:T(8,128)(2,1)S(1)} %get-tuple-element.5), channel_id=1, source_target_pairs={{0,1},{1,2},{2,3},{3,4},{4,5},{5,6},{6,7},{7,8},{8,9},{9,10},{10,1... | collective-permute-start | bytes 1572872 | tf_op jit(solution)/shard_map/ppermute | solution.py:12
  107.5 1.9 %collective-permute-start.3 = (bf16[32,64,128]{2,1,0:T(8,128)(2,1)S(1)}, bf16[32,64,128]{2,1,0:T(8,128)(2,1)}, u32[]{:S(2)}, u32[]{:S(2)}) collective-permute-start(bf16[32,64,128]{2,1,0:T(8,128)(2,1)S(1)} %get-tuple-element.6), channel_id=1, source_target_pairs={{1,0},{2,1},{3,2},{4,3},{5,4},{6,5},{7,6},{8,7},{9,8},{10,9},{11,1... | collective-permute-start | bytes 1572872 | tf_op jit(solution)/shard_map/ppermute | solution.py:15
  109.4 2.9 %all-to-all-done.1 = bf16[128,2,256]{2,1,0:T(2,128)(2,1)S(1)} async-done(((bf16[128,2,256]{2,1,0:T(2,128)(2,1)}), bf16[128,2,256]{2,1,0:T(2,128)(2,1)S(1)}, u32[]{:S(2)}, u32[]{:S(2)}) %all-to-all-start.1) | async-done | bytes 131104 | tf_op jit(solution)/shard_map/all_to_all | solution.py:70
  112.4 0.1 convert_multiply_fusion
  112.5 0.2 reshape.38
  112.7 0.4 convolution_convert_fusion
  113.1 0.5 collective-permute-done.2
  113.6 4.5 %collective-permute-done.3 = bf16[32,64,128]{2,1,0:T(8,128)(2,1)} collective-permute-done((bf16[32,64,128]{2,1,0:T(8,128)(2,1)S(1)}, bf16[32,64,128]{2,1,0:T(8,128)(2,1)}, u32[]{:S(2)}, u32[]{:S(2)}) %collective-permute-start.3) | collective-permute-done | bytes 524320 | tf_op jit(solution)/shard_map/ppermute | solution.py:15
  118.1 7.4 %fusion.27 = bf16[576,8,128]{2,1,0:T(8,128)(2,1)S(1)} fusion(bf16[32,64,128]{2,1,0:T(8,128)(2,1)} %collective-permute-done.3, bf16[512,63,128]{2,1,0:T(8,128)(2,1)} %bitcast.63, bf16[512,1,128]{2,1,0:T(2,128)(2,1)S(1)} %copy.21, bf16[32,64,128]{2,1,0:T(8,128)(2,1)} %collective-permute-done.2, bf16[8,64]{1,0:T(8,128)(2,1)S(1)} %copy-done.6), kind=kOutput, calls=%fused_computation.30 | convolution fusion | flops 113836032 | bytes 10617856 | tf_op jit(solution)/shard_map/jh,shb->sjb/dot_general | solution.py:55
  125.5 20.7 %gather_fusion.2 = bf16[4096,128]{1,0:T(8,128)(2,1)S(1)} fusion(bf16[576,8,128]{2,1,0:T(8,128)(2,1)S(1)} %fusion.27, s32[4096]{0:T(1024)S(1)} %reshape.40), kind=kCustom, calls=%fused_computation.2 | custom fusion | bytes 2129920 | tf_op jit(solution)/shard_map/gather | solution.py:58
  146.3 1.4 fusion.43
  147.7 0.4 convolution_bitcast_fusion
  148.1 0.8 pad_maximum_fusion.1
  (3 shorter events, 0.0 us)
Async XLA Ops:
  0.0 66.5 %copy-start = (bf16[8,128,128]{2,1,0:T(8,128)(2,1)S(1)}, bf16[8,128,128]{2,1,0:T(8,128)(2,1)}, u32[]{:S(2)}) copy-start(bf16[8,128,128]{2,1,0:T(8,128)(2,1)} %param.13) | copy-start | bytes 786436
  1.8 29.8 %copy-start.4 = (s32[512,8]{0,1:T(8,128)S(1)}, s32[512,8]{0,1:T(8,128)}, u32[]{:S(2)}) copy-start(s32[512,8]{0,1:T(8,128)} %param.18) | copy-start | bytes 49156
  1.8 29.8 %copy-start.5 = (s32[1,128,2]{1,2,0:T(2,128)S(1)}, s32[1,128,2]{1,2,0:T(2,128)}, u32[]{:S(2)}) copy-start(s32[1,128,2]{1,2,0:T(2,128)} %param.20) | copy-start | bytes 3076
  1.8 33.0 %copy-start.1 = (bf16[1,128,2,256]{3,2,1,0:T(2,128)(2,1)S(1)}, bf16[1,128,2,256]{3,2,1,0:T(2,128)(2,1)}, u32[]{:S(2)}) copy-start(bf16[1,128,2,256]{3,2,1,0:T(2,128)(2,1)} %param.21) | copy-start | bytes 393220
  1.9 38.3 %copy-start.6 = (bf16[8,64]{1,0:T(8,128)(2,1)S(1)}, bf16[8,64]{1,0:T(8,128)(2,1)}, u32[]{:S(2)}) copy-start(bf16[8,64]{1,0:T(8,128)(2,1)} %param.12) | copy-start | bytes 3076
  13.3 21.5 %all-to-all-start = ((bf16[128,2,256]{2,1,0:T(2,128)(2,1)}), bf16[128,2,256]{2,1,0:T(2,128)(2,1)S(1)}, u32[]{:S(2)}, u32[]{:S(2)}) async-start(bf16[128,2,256]{2,1,0:T(2,128)(2,1)} %broadcast_select_fusion.1), calls=%async_computation | async-start | bytes 262144 | tf_op jit(solution)/shard_map/all_to_all | solution.py:70
  26.1 9.7 %collective-permute-start = (bf16[32,64,128]{2,1,0:T(8,128)(2,1)S(1)}, bf16[32,64,128]{2,1,0:T(8,128)(2,1)S(1)}, u32[]{:S(2)}, u32[]{:S(2)}) collective-permute-start(bf16[32,64,128]{2,1,0:T(8,128)(2,1)S(1)} %get-tuple-element.7), channel_id=1, source_target_pairs={{0,1},{1,2},{2,3},{3,4},{4,5},{5,6},{6,7},{7,8},{8,9},{9,10},{10,1... | collective-permute-start | bytes 1572872 | tf_op jit(solution)/shard_map/ppermute | solution.py:12
  29.6 10.5 %collective-permute-start.1 = (bf16[32,64,128]{2,1,0:T(8,128)(2,1)S(1)}, bf16[32,64,128]{2,1,0:T(8,128)(2,1)S(1)}, u32[]{:S(2)}, u32[]{:S(2)}) collective-permute-start(bf16[32,64,128]{2,1,0:T(8,128)(2,1)S(1)} %get-tuple-element.8), channel_id=1, source_target_pairs={{1,0},{2,1},{3,2},{4,3},{5,4},{6,5},{7,6},{8,7},{9,8},{10,9},{11,1... | collective-permute-start | bytes 1572872 | tf_op jit(solution)/shard_map/ppermute | solution.py:15
  45.5 22.3 %copy-start.2 = (bf16[256,128]{1,0:T(8,128)(2,1)S(1)}, bf16[256,128]{1,0:T(8,128)(2,1)}, u32[]{:S(2)}) copy-start(bf16[256,128]{1,0:T(8,128)(2,1)} %param.15) | copy-start | bytes 196612
  45.5 22.3 %copy-start.3 = (bf16[128,128]{1,0:T(8,128)(2,1)S(1)}, bf16[128,128]{1,0:T(8,128)(2,1)}, u32[]{:S(2)}) copy-start(bf16[128,128]{1,0:T(8,128)(2,1)} %param.16) | copy-start | bytes 98308
  91.4 20.9 %all-to-all-start.1 = ((bf16[128,2,256]{2,1,0:T(2,128)(2,1)}), bf16[128,2,256]{2,1,0:T(2,128)(2,1)S(1)}, u32[]{:S(2)}, u32[]{:S(2)}) async-start(bf16[128,2,256]{2,1,0:T(2,128)(2,1)} %broadcast_select_fusion), calls=%async_computation.1 | async-start | bytes 262144 | tf_op jit(solution)/shard_map/all_to_all | solution.py:70
  103.9 9.7 %collective-permute-start.2 = (bf16[32,64,128]{2,1,0:T(8,128)(2,1)S(1)}, bf16[32,64,128]{2,1,0:T(8,128)(2,1)}, u32[]{:S(2)}, u32[]{:S(2)}) collective-permute-start(bf16[32,64,128]{2,1,0:T(8,128)(2,1)S(1)} %get-tuple-element.5), channel_id=1, source_target_pairs={{0,1},{1,2},{2,3},{3,4},{4,5},{5,6},{6,7},{7,8},{8,9},{9,10},{10,1... | collective-permute-start | bytes 1572872 | tf_op jit(solution)/shard_map/ppermute | solution.py:12
  107.5 10.6 %collective-permute-start.3 = (bf16[32,64,128]{2,1,0:T(8,128)(2,1)S(1)}, bf16[32,64,128]{2,1,0:T(8,128)(2,1)}, u32[]{:S(2)}, u32[]{:S(2)}) collective-permute-start(bf16[32,64,128]{2,1,0:T(8,128)(2,1)S(1)} %get-tuple-element.6), channel_id=1, source_target_pairs={{1,0},{2,1},{3,2},{4,3},{5,4},{6,5},{7,6},{8,7},{9,8},{10,9},{11,1... | collective-permute-start | bytes 1572872 | tf_op jit(solution)/shard_map/ppermute | solution.py:15
where the time goes:
time: 151 us; the launch traced here: 149 us
  local copies, waits for them, and re-layouts  46.9 us (31%)
  matrix products  35.8 us (24%)
  starting transfers between devices  33.3 us (22%)
  other arithmetic  17.5 us (12%)
  waiting for transfers between devices  15.2 us (10%)
    gather x2, local copies, waits for them, and re-layouts, body(): picked = reduced[local_neighbours, slot_ids[None, :], :]  41.7 us
    all_to_all x2, starting transfers between devices, body(): lax.all_to_all(outbound, ('group', 'member'), split_axis=0, concat_axis=0...  22.4 us
    dot_general x2, matrix products, body(): jnp.dot(history.reshape(cluster_count, history_depth * basis_width), proj...  18.6 us
    concatenate x2, other arithmetic, body(): jnp.concatenate([current.astype(jnp.bfloat16)[:, None], history[:, :histo...  13.1 us
    dot_general x2, matrix products, body(): jnp.einsum('jh,shb->sjb', near_time, extended, preferred_element_type=jnp...  12.8 us
    ppermute x2, waiting for transfers between devices, padded(): lax.ppermute(lax.slice_in_dim(block, 0, width, axis=dim), axis, backward)  8.9 us
    ppermute x2, starting transfers between devices, padded(): lax.ppermute(lax.slice_in_dim(block, block.shape[dim] - width, None, axis...  7.08 us
    all_to_all x2, waiting for transfers between devices, body(): lax.all_to_all(outbound, ('group', 'member'), split_axis=0, concat_axis=0...  5.61 us
  transfers between devices with their start and end apart: 6, of which 6 were waited for; matrix products, arithmetic and copies ran while one was open for 3% of the time, Pallas kernels for 0%

commit v1 on v0

v1 whole, which is shorter than its diff:
```python
import functools

import jax
import jax.numpy as jnp
from jax import lax
from jax.experimental import pallas as pl
from jax.experimental.pallas import tpu as pltpu
from jax.sharding import PartitionSpec as P

MESH = pl.DeviceIdType.MESH
BF16 = jnp.bfloat16
F32 = jnp.float32

CL = 512
NB = 128
H = 64
K = 256
NNB = 8
RIM = 32
GROUPS = 4
MEMBERS = 32
HC = 16
NQ = H // HC
ROWS = 3 * MEMBERS * 2
PAIRS = GROUPS * MEMBERS * 2
EXT = CL + 2 * RIM
BLK = 128
WIN = BLK + 2 * RIM


def dot(a, b):
    return jnp.dot(a, b, preferred_element_type=F32)


def iota(shape, dim):
    return lax.broadcasted_iota(jnp.int32, shape, dim)


def one_hot(mask):
    return jnp.where(mask, 1.0, 0.0).astype(BF16)


def far_offsets():
    dist = (0, 1, 2, 1)
    offsets = [
        (dz, dy, dx, dc) for dz in (2, 1, 3) for dy in range(4) for dx in range(4) for dc in (1, 0)
    ]
    return sorted(offsets, key=lambda o: -(dist[o[0]] + dist[o[1]] + dist[o[2]]))


def kernel(
    src_hbm,
    obs_hbm,
    hist_hbm,
    ntime_hbm,
    nkern_hbm,
    proj_hbm,
    rmap_hbm,
    sinv_hbm,
    inc_hbm,
    nbr_hbm,
    trans_hbm,
    out_hbm,
    src,
    obs,
    hv0,
    hv1,
    hv2,
    hv3,
    ntime,
    nkern,
    pv,
    rmap,
    sinv,
    inc,
    nbr,
    trans,
    cur,
    arows,
    part1,
    perm,
    gone,
    oone,
    sone,
    mone,
    tt,
    rext,
    r1p,
    base,
    outb,
    inb,
    load_sem,
    hist_sem,
    proj_sem,
    send_sem,
    recv_sem,
    halo_send,
    halo_recv,
    out_sem,
):
    g = lax.axis_index("group")
    m = lax.axis_index("member")
    me = g * MEMBERS + m
    z, y, x, c = g, m // 8, (m // 2) % 4, m % 2
    right = (m + 1) % MEMBERS
    left = (m + MEMBERS - 1) % MEMBERS

    def peer(o):
        dz, dy, dx, dc = o
        return (z + dz) % 4, ((y + dy) % 4) * 8 + ((x + dx) % 4) * 2 + (c + dc) % 2

    hv = (hv0, hv1, hv2, hv3)

    small = []

    def load(i, a, b):
        cp = pltpu.make_async_copy(a, b, load_sem.at[i])
        cp.start()
        small.append(cp)

    load(0, src_hbm, src)
    load(1, obs_hbm, obs)
    load(2, nbr_hbm, nbr)
    load(3, ntime_hbm, ntime)
    hist_cp = []
    proj_cp = []
    for q in range(NQ):
        cp = pltpu.make_async_copy(hist_hbm.at[:, pl.ds(q * HC, HC)], hv[q], hist_sem.at[q])
        cp.start()
        hist_cp.append(cp)
        cp = pltpu.make_async_copy(
            proj_hbm.at[pl.ds(q * HC * NB, HC * NB)], pv.at[pl.ds(q * HC * NB, HC * NB)], proj_sem.at[q]
        )
        cp.start()
        proj_cp.append(cp)
    load(4, nkern_hbm, nkern)
    load(5, inc_hbm, inc)
    load(6, trans_hbm, trans)
    load(7, rmap_hbm, rmap)
    load(8, sinv_hbm, sinv)

    barrier = pltpu.get_barrier_semaphore()
    for o in far_offsets():
        pl.semaphore_signal(barrier, inc=1, device_id=peer(o), device_id_type=MESH)
    pl.semaphore_signal(barrier, inc=1, device_id=(g, right), device_id_type=MESH)
    pl.semaphore_signal(barrier, inc=1, device_id=(g, left), device_id_type=MESH)

    r = iota((256, 256), 0)
    perm[...] = one_hot(iota((256, 256), 1) == (r % 16) * 16 + r // 16)
    for t in range(2):
        inb[t, :, pl.ds(g * MEMBERS, MEMBERS)] = jnp.zeros((2, MEMBERS, 2, 128), BF16)
    for cp in small[:4]:
        cp.wait()

    tn = ntime[...]
    rr = iota((128, NNB), 0)
    pick = one_hot((rr // 8) % 8 == iota((128, NNB), 1))
    wide = dot(pick, tn).astype(BF16)
    cols = iota((H, 512), 1)
    step = (cols // 128) * 16 + cols % 16
    same = one_hot(iota((H, 512), 0) == step)
    shifted = one_hot(iota((H, 512), 0) == step + 1)
    tr = iota((128, 512), 0)
    tc = iota((128, 512), 1)
    keep = tr % 8 == (tc // 16) % 8
    table = jnp.where(tr < 64, dot(wide, same), dot(wide, shifted))
    tt[...] = jnp.where(keep, table, 0.0).astype(BF16)

    oone[...] = one_hot(iota((CL, PAIRS), 0) == obs[...])
    sub = iota((8, CL), 0)
    lane = iota((8, CL), 1)

    def source_rows(i, carry):
        d = i // 8
        first = ((g + d + 1) % GROUPS) * 64 + (i % 8) * 8
        want = jnp.full((8, CL), -1, jnp.int32)
        for k in range(8):
            want = jnp.where(sub == k, src[first + k], want)
        sone[pl.ds(pl.multiple_of(i * 8, 8), 8), :] = jnp.where(lane == want, 1.0, 0.0)
        return carry

    lax.fori_loop(0, ROWS // 8, source_rows, 0)

    wl = iota((BLK, WIN), 1)
    for blk in range(CL // BLK):
        off = me * CL + blk * BLK - RIM
        for j in range(NNB):
            col = nbr[pl.ds(blk * BLK, BLK), j : j + 1] - off
            gone[blk, j] = one_hot(wl == col)

    acc = jnp.zeros((ROWS, K), F32)
    for q in range(NQ):
        hist_cp[q].wait()

        def gather(i, carry):
            d = i // 2
            first = ((g + d + 1) % GROUPS) * 64 + (i % 2) * 32
            parts = [hv[q][jnp.maximum(src[first + k], 0)] for k in range(32)]
            tile = jnp.concatenate(
                [jnp.concatenate(parts[:16], axis=0), jnp.concatenate(parts[16:], axis=0)], axis=1
            )
            turned = dot(perm[...], tile).astype(BF16)
            for h in range(HC):
                for s in range(2):
                    arows[
                        pl.ds(pl.multiple_of(i * 32 + s * 16, 16), 16), pl.ds((q * HC + h) * NB, NB)
                    ] = turned[h * 16 : (h + 1) * 16, s * NB : (s + 1) * NB]
            return carry

        lax.fori_loop(0, ROWS // 32, gather, 0)
        proj_cp[q].wait()
        acc = acc + dot(
            arows[:, pl.ds(q * HC * NB, HC * NB)], pv[pl.ds(q * HC * NB, HC * NB), :]
        )

    def store_rays(t, rows):
        flat = outb.at[t].reshape(2, ROWS, 128)
        flat[0] = rows[:, :NB]
        flat[1] = rows[:, NB:]

    def send_rays(t):
        for o in far_offsets():
            gg, mm = peer(o)
            pltpu.make_async_remote_copy(
                outb.at[t, :, (o[0] - 1) * MEMBERS + mm],
                inb.at[t, :, me],
                send_sem.at[t],
                recv_sem.at[t],
                device_id=(gg, mm),
                device_id_type=MESH,
            ).start()

    def wait_rays(t):
        part = inb.at[t, :, pl.ds(0, ROWS // 2)]
        pltpu.make_async_copy(part, part, recv_sem.at[t]).wait()

    def halo(t, side):
        if side == 0:
            return pltpu.make_async_remote_copy(
                rext.at[t, :, pl.ds(CL, RIM)],
                rext.at[t, :, pl.ds(0, RIM)],
                halo_send.at[t, 0],
                halo_recv.at[t, 0],
                device_id=(g, right),
                device_id_type=MESH,
            )
        return pltpu.make_async_remote_copy(
            rext.at[t, :, pl.ds(RIM, RIM)],
            rext.at[t, :, pl.ds(RIM + CL, RIM)],
            halo_send.at[t, 1],
            halo_recv.at[t, 1],
            device_id=(g, left),
            device_id_type=MESH,
        )

    outgoing = acc.astype(BF16)
    store_rays(0, outgoing)
    pl.semaphore_wait(barrier, 3 * MEMBERS + 2)
    send_rays(0)

    def reduce_group(i, carry):
        halves = []
        for s in range(2):
            first = pl.multiple_of(i * 16 + s * 8, 8)
            halves.append(
                jnp.concatenate([hv[q][pl.ds(first, 8)].reshape(128, NB) for q in range(NQ)], axis=0)
            )
        red = dot(tt[...], jnp.concatenate(halves, axis=1))
        at = pl.multiple_of(i * 16, 16)
        for j in range(NNB):
            a = red[j * 8 : j * 8 + 8]
            rext[0, j, pl.ds(pl.multiple_of(at + RIM, 16), 16), :] = jnp.concatenate(
                [a[:, :NB], a[:, NB:]], axis=0
            ).astype(BF16)
            b = red[64 + j * 8 : 72 + j * 8]
            r1p[j, pl.ds(at, 16), :] = jnp.concatenate([b[:, :NB], b[:, NB:]], axis=0)
        return carry

    for i in (0, 1, 30, 31):
        reduce_group(i, 0)
    halo(0, 0).start()
    halo(0, 1).start()
    lax.fori_loop(2, 30, reduce_group, 0)

    part1[...] = dot(arows[:, : (H - 1) * NB], pv[NB:, :])
    mone[...] = dot(sone[...].astype(BF16), oone[...]).astype(BF16)

    for cp in small[4:]:
        cp.wait()

    def near_block(t, blk):
        picked = [
            dot(gone[blk, j], rext[t, j, pl.ds(blk * BLK, WIN), :]).astype(BF16) for j in range(NNB)
        ]
        near = dot(jnp.concatenate(picked, axis=1), nkern[...])
        base[pl.ds(blk * BLK, BLK), :] = inc[t, pl.ds(blk * BLK, BLK), :] - near

    def near_field(t):
        near_block(t, 1)
        near_block(t, 2)
        halo(t, 0).wait_recv()
        near_block(t, 0)
        halo(t, 1).wait_recv()
        near_block(t, 3)

    def contributions(t):
        halves = [trans[s].astype(F32) * inb.at[t].reshape(2, PAIRS, 128)[s].astype(F32) for s in range(2)]
        full = jnp.concatenate(halves, axis=1)
        high = full.astype(BF16)
        low = (full - high.astype(F32)).astype(BF16)
        return high, low

    near_field(0)
    full = base[...]
    b0 = full.astype(BF16)
    rest = full - b0.astype(F32)
    b1 = rest.astype(BF16)
    b2 = (rest - b1.astype(F32)).astype(BF16)
    sel = sone[...].astype(BF16)
    base_src = dot(sel, b0) + dot(sel, b1) + dot(sel, b2)

    wait_rays(0)
    high, low = contributions(0)

    def currents(hot, start):
        incoming = (dot(hot, high) + dot(hot, low)).astype(BF16)
        rhs = (start - dot(incoming, rmap[...])).astype(BF16)
        return dot(rhs, sinv[...])

    at_src = currents(mone[...], base_src).astype(BF16)
    outgoing = (part1[...] + dot(at_src, pv[:NB, :])).astype(BF16)
    store_rays(1, outgoing)
    send_rays(1)

    cur0 = currents(oone[...], base[...])
    cur[0] = cur0
    out0 = pltpu.make_async_copy(cur.at[0], out_hbm.at[0], out_sem.at[0])
    out0.start()
    newest = cur0.astype(BF16).astype(F32)
    for j in range(NNB):
        weight = ntime[j : j + 1, 0:1].astype(F32)
        rext[1, j, pl.ds(RIM, CL), :] = (r1p[j] + weight * newest).astype(BF16)
    halo(1, 0).start()
    halo(1, 1).start()
    near_field(1)

    wait_rays(1)
    high, low = contributions(1)
    cur[1] = currents(oone[...], base[...])
    out1 = pltpu.make_async_copy(cur.at[1], out_hbm.at[1], out_sem.at[1])
    out1.start()
    for t in range(2):
        halo(t, 0).wait_send()
        halo(t, 1).wait_send()
        pltpu.make_async_copy(outb.at[t], outb.at[t], send_sem.at[t]).wait()
    out0.wait()
    out1.wait()


def body(
    history,
    near_time,
    near_kernel,
    projection,
    receive_map,
    self_inverse,
    incident,
    neighbours,
    send_sources,
    recv_observers,
    transfer,
):
    halves = transfer.reshape(PAIRS, 2, 128).swapaxes(0, 1)
    args = (
        send_sources.reshape(PAIRS),
        recv_observers.reshape(1, PAIRS),
        history,
        near_time,
        near_kernel.reshape(NNB * NB, NB),
        projection.reshape(H * NB, K),
        receive_map,
        self_inverse,
        incident,
        neighbours,
        halves,
    )
    scratch = [
        pltpu.SMEM((PAIRS,), jnp.int32),
        pltpu.VMEM((1, PAIRS), jnp.int32),
        *[pltpu.VMEM((CL, HC, NB), BF16) for _ in range(NQ)],
        pltpu.VMEM((NNB, H), BF16),
        pltpu.VMEM((NNB * NB, NB), BF16),
        pltpu.VMEM((H * NB, K), BF16),
        pltpu.VMEM((K, NB), BF16),
        pltpu.VMEM((NB, NB), BF16),
        pltpu.VMEM((2, CL, NB), F32),
        pltpu.VMEM((CL, NNB), jnp.int32),
        pltpu.VMEM((2, PAIRS, 128), BF16),
        pltpu.VMEM((2, CL, NB), F32),
        pltpu.VMEM((ROWS, H * NB), BF16),
        pltpu.VMEM((ROWS, K), F32),
        pltpu.VMEM((256, 256), BF16),
        pltpu.VMEM((CL // BLK, NNB, BLK, WIN), BF16),
        pltpu.VMEM((CL, PAIRS), BF16),
        pltpu.VMEM((ROWS, CL), F32),
        pltpu.VMEM((ROWS, PAIRS), BF16),
        pltpu.VMEM((128, 512), BF16),
        pltpu.VMEM((2, NNB, EXT, NB), BF16),
        pltpu.VMEM((NNB, CL, NB), F32),
        pltpu.VMEM((CL, NB), F32),
        pltpu.VMEM((2, 2, ROWS // 2, 2, 128), BF16),
        pltpu.VMEM((2, 2, PAIRS // 2, 2, 128), BF16),
        pltpu.SemaphoreType.DMA((9,)),
        pltpu.SemaphoreType.DMA((NQ,)),
        pltpu.SemaphoreType.DMA((NQ,)),
        pltpu.SemaphoreType.DMA((2,)),
        pltpu.SemaphoreType.DMA((2,)),
        pltpu.SemaphoreType.DMA((2, 2)),
        pltpu.SemaphoreType.DMA((2, 2)),
        pltpu.SemaphoreType.DMA((2,)),
    ]
    return pl.pallas_call(
        kernel,
        out_shape=jax.ShapeDtypeStruct((2, CL, NB), F32),
        in_specs=[pl.BlockSpec(memory_space=pl.ANY)] * len(args),
        out_specs=pl.BlockSpec(memory_space=pl.ANY),
        scratch_shapes=scratch,
        compiler_params=pltpu.CompilerParams(
            collective_id=0, has_side_effects=True, vmem_limit_bytes=50 << 20
        ),
        cost_estimate=pl.CostEstimate(
            flops=4_000_000_000, bytes_accessed=14 << 20, transcendentals=0
        ),
    )(*args)


def solution(mesh):
    both = ("group", "member")
    in_specs = (
        P(both, None, None),
        P(),
        P(),
        P(),
        P(),
        P(),
        P(None, both, None),
        P(both, None),
        P(both, None, None),
        P(both, None, None),
        P(both, None, None, None),
    )
    out_specs = P(None, both, None)
    return jax.shard_map(body, mesh=mesh, in_specs=in_specs, out_specs=out_specs, check_vma=False)
```

time: 151 us -> 43 us (0.28); the launches traced: 149 us -> 42.6 us
  local copies, waits for them, and re-layouts: 46.9 us -> 8.77 us
  matrix products: 35.8 us -> 0 us
  Pallas kernels: 0 us -> 33.8 us
  starting transfers between devices: 33.3 us -> 0 us
  other arithmetic: 17.5 us -> 0 us
  waiting for transfers between devices: 15.2 us -> 0 us
    gather x6 -> x0, local copies, waits for them, and re-layouts: 44.1 us -> none  [the longest x2 41.7 us: body(): picked = reduced[local_neighbours, slot_ids[None, :], :]]
    dot_general x10 -> x0, matrix products: 35.8 us -> none  [the longest x2 18.6 us: body(): jnp.dot(history.reshape(cluster_count, history_depth * basis_width), proj...]
    pallas_call x0 -> x1, Pallas kernels: none -> 33.8 us  [body(): pl.pallas_call(kernel, out_shape=jax.ShapeDtypeStruct((2, CL, NB), F32),...]
    all_to_all x2 -> x0, starting transfers between devices: 22.4 us -> none  [body(): lax.all_to_all(outbound, ('group', 'member'), split_axis=0, concat_axis=0...]
    concatenate x3 -> x0, other arithmetic: 13.2 us -> none  [the longest x2 13.1 us: body(): jnp.concatenate([current.astype(jnp.bfloat16)[:, None], history[:, :histo...]
    ppermute x4 -> x0, starting transfers between devices: 10.9 us -> none  [the longest x2 7.08 us: padded(): lax.ppermute(lax.slice_in_dim(block, block.shape[dim] - width, None, axis...]
    ppermute x4 -> x0, waiting for transfers between devices: 9.55 us -> none  [the longest x2 8.9 us: padded(): lax.ppermute(lax.slice_in_dim(block, 0, width, axis=dim), axis, backward)]
    unnamed x15 -> x14, local copies, waits for them, and re-layouts: 0.15 us -> 7.48 us
  transfers between devices with their start and end apart: 6 -> 0, of which waited for: 6 -> 0; matrix products, arithmetic and copies ran while one was open for 3% -> 0% of each run, Pallas kernels for 0% -> 0%
where the time goes in v1:
time: 43 us; the launch traced here: 42.6 us
  Pallas kernels  33.8 us (79%)
  local copies, waits for them, and re-layouts  8.77 us (20%)
    pallas_call x1, Pallas kernels, body(): pl.pallas_call(kernel, out_shape=jax.ShapeDtypeStruct((2, CL, NB), F32),...  33.8 us
    unnamed x14, local copies, waits for them, and re-layouts  7.48 us
    reshape x2, local copies, waits for them, and re-layouts, body(): halves = transfer.reshape(PAIRS, 2, 128).swapaxes(0, 1)  1.02 us

profile of v1, /device:TPU:1, one launch (start us, length us, event | category | flops | bytes accessed | tf_op | source)
XLA Modules:
  0.0 42.6 jit_solution(7536269111941496454)
XLA Ops:
  0.0 0.8 %copy.14 = s32[1,128,2]{2,1,0:T(8,128)S(1)} copy(s32[1,128,2]{1,2,0:T(2,128)} %param.19) | data formatting | bytes 2048 | tf_op args[8]
  0.8 0.1 reshape.15.src_hbm
  0.9 0.8 %copy.15 = s32[1,128,2]{2,1,0:T(8,128)S(1)} copy(s32[1,128,2]{1,2,0:T(2,128)} %param.20) | data formatting | bytes 2048 | tf_op args[9]
  1.7 0.1 reshape.16.obs_hbm
  1.9 1.0 %reshape.19 = bf16[256,2,128]{2,1,0:T(2,128)(2,1)S(1)} reshape(bf16[1,128,2,256]{3,2,1,0:T(2,128)(2,1)} %param.21) | data formatting | bytes 262144 | tf_op jit(solution)/shard_map/reshape | solution.py:373
  2.9 0.8 %copy.17.nbr_hbm = s32[512,8]{1,0:T(8,128)S(1)} copy(s32[512,8]{0,1:T(8,128)} %param.18) | data formatting | bytes 32768 | tf_op args[7]
  3.7 0.0 copy-start
  3.7 1.0 %copy-done = f32[2,512,128]{2,1,0:T(8,128)S(1)} copy-done((f32[2,512,128]{2,1,0:T(8,128)S(1)}, f32[2,512,128]{2,1,0:T(8,128)}, u32[]{:S(2)}) %copy-start) | copy-done | bytes 524312
  4.8 0.0 copy-start.1
  4.8 0.9 %copy-done.1 = bf16[8,128,128]{2,1,0:T(8,128)(2,1)S(1)} copy-done((bf16[8,128,128]{2,1,0:T(8,128)(2,1)S(1)}, bf16[8,128,128]{2,1,0:T(8,128)(2,1)}, u32[]{:S(2)}) %copy-start.1) | copy-done | bytes 262168
  5.7 0.0 copy-start.2
  5.7 0.8 %copy-done.2 = bf16[256,128]{1,0:T(8,128)(2,1)S(1)} copy-done((bf16[256,128]{1,0:T(8,128)(2,1)S(1)}, bf16[256,128]{1,0:T(8,128)(2,1)}, u32[]{:S(2)}) %copy-start.2) | copy-done | bytes 65560
  6.6 0.0 copy-start.3
  6.6 0.8 %copy-done.3 = bf16[128,128]{1,0:T(8,128)(2,1)S(1)} copy-done((bf16[128,128]{1,0:T(8,128)(2,1)S(1)}, bf16[128,128]{1,0:T(8,128)(2,1)}, u32[]{:S(2)}) %copy-start.3) | copy-done | bytes 32792
  7.3 0.0 copy-start.4
  7.3 0.7 %copy-done.4 = bf16[8,64]{1,0:T(8,128)(2,1)S(1)} copy-done((bf16[8,64]{1,0:T(8,128)(2,1)S(1)}, bf16[8,64]{1,0:T(8,128)(2,1)}, u32[]{:S(2)}) %copy-start.4) | copy-done | bytes 1048
  8.0 33.8 %shard_map.109 = f32[2,512,128]{2,1,0:T(8,128)S(1)} custom-call(s32[256]{0:T(256)S(1)} %reshape.15.src_hbm, s32[1,256]{1,0:T(1,128)S(1)} %reshape.16.obs_hbm, bf16[512,64,128]{2,1,0:T(8,128)(2,1)} %hist_hbm.1, bf16[8,64]{1,0:T(8,128)(2,1)S(1)} %copy-done.4, bf16[1024,128]{1,0:T(8,128)(2,1)S(1)} %bitcast.6, bf16[8192,256]{1,0:T(8,128)(2,1)} %bitcast.7, ...), custom_call_target="tpu_custom_call" | custom-call | flops 4000000000 | bytes 14680064 | tf_op jit(solution)/shard_map/pallas_call | solution.py:422
  41.8 0.8 %copy.21 = f32[2,512,128]{2,1,0:T(8,128)} copy(f32[2,512,128]{2,1,0:T(8,128)S(1)} %shard_map.109) | data formatting | bytes 1048576
  (1 shorter events, 0.0 us)
Async XLA Ops:
  3.7 1.0 %copy-start = (f32[2,512,128]{2,1,0:T(8,128)S(1)}, f32[2,512,128]{2,1,0:T(8,128)}, u32[]{:S(2)}) copy-start(f32[2,512,128]{2,1,0:T(8,128)} %inc_hbm.1) | copy-start | bytes 1572868
  4.8 0.9 %copy-start.1 = (bf16[8,128,128]{2,1,0:T(8,128)(2,1)S(1)}, bf16[8,128,128]{2,1,0:T(8,128)(2,1)}, u32[]{:S(2)}) copy-start(bf16[8,128,128]{2,1,0:T(8,128)(2,1)} %param.13) | copy-start | bytes 786436
  5.7 0.8 %copy-start.2 = (bf16[256,128]{1,0:T(8,128)(2,1)S(1)}, bf16[256,128]{1,0:T(8,128)(2,1)}, u32[]{:S(2)}) copy-start(bf16[256,128]{1,0:T(8,128)(2,1)} %rmap_hbm.1) | copy-start | bytes 196612
  6.6 0.8 %copy-start.3 = (bf16[128,128]{1,0:T(8,128)(2,1)S(1)}, bf16[128,128]{1,0:T(8,128)(2,1)}, u32[]{:S(2)}) copy-start(bf16[128,128]{1,0:T(8,128)(2,1)} %sinv_hbm.1) | copy-start | bytes 98308
  7.3 0.7 %copy-start.4 = (bf16[8,64]{1,0:T(8,128)(2,1)S(1)}, bf16[8,64]{1,0:T(8,128)(2,1)}, u32[]{:S(2)}) copy-start(bf16[8,64]{1,0:T(8,128)(2,1)} %ntime_hbm.1) | copy-start | bytes 3076

commit v2 on v1

--- a/solution.py
+++ b/solution.py
@@ -19,12 +19,14 @@
 RIM = 32
 GROUPS = 4
 MEMBERS = 32
+DEVICES = GROUPS * MEMBERS
 HC = 16
 NQ = H // HC
 ROWS = 3 * MEMBERS * 2
 PAIRS = GROUPS * MEMBERS * 2
 EXT = CL + 2 * RIM
 BLK = 128
+UNROLL = 6
 WIN = BLK + 2 * RIM
 
 
@@ -60,7 +62,7 @@
     inc_hbm,
     nbr_hbm,
     trans_hbm,
-    out_hbm,
+    out,
     src,
     obs,
     hv0,
@@ -75,7 +77,6 @@
     inc,
     nbr,
     trans,
-    cur,
     arows,
     part1,
     perm,
@@ -96,7 +97,6 @@
     recv_sem,
     halo_send,
     halo_recv,
-    out_sem,
 ):
     g = lax.axis_index("group")
     m = lax.axis_index("member")
@@ -135,9 +135,10 @@
         proj_cp.append(cp)
     load(4, nkern_hbm, nkern)
     load(5, inc_hbm, inc)
-    load(6, trans_hbm, trans)
-    load(7, rmap_hbm, rmap)
-    load(8, sinv_hbm, sinv)
+    load(6, trans_hbm.at[:, :, pl.ds(0, 128)], trans.at[0])
+    load(7, trans_hbm.at[:, :, pl.ds(128, 128)], trans.at[1])
+    load(8, rmap_hbm, rmap)
+    load(9, sinv_hbm, sinv)
 
     barrier = pltpu.get_barrier_semaphore()
     for o in far_offsets():
@@ -166,16 +167,21 @@
     table = jnp.where(tr < 64, dot(wide, same), dot(wide, shifted))
     tt[...] = jnp.where(keep, table, 0.0).astype(BF16)
 
-    oone[...] = one_hot(iota((CL, PAIRS), 0) == obs[...])
+    seen = obs[...]
+    own = iota((CL, DEVICES), 0)
+    by_slot = jnp.concatenate([one_hot(own == seen[s : s + 1]) for s in range(2)], axis=1)
+    r = iota((PAIRS, PAIRS), 0)
+    weave = one_hot(iota((PAIRS, PAIRS), 1) == (r % DEVICES) * 2 + r // DEVICES)
+    oone[...] = dot(by_slot, weave).astype(BF16)
     sub = iota((8, CL), 0)
     lane = iota((8, CL), 1)
 
     def source_rows(i, carry):
         d = i // 8
-        first = ((g + d + 1) % GROUPS) * 64 + (i % 8) * 8
+        first = ((g + d + 1) % GROUPS) * MEMBERS + (i % 8) * 4
         want = jnp.full((8, CL), -1, jnp.int32)
         for k in range(8):
-            want = jnp.where(sub == k, src[first + k], want)
+            want = jnp.where(sub == k, src[k % 2, first + k // 2], want)
         sone[pl.ds(pl.multiple_of(i * 8, 8), 8), :] = jnp.where(lane == want, 1.0, 0.0)
         return carry
 
@@ -184,30 +190,35 @@
     wl = iota((BLK, WIN), 1)
     for blk in range(CL // BLK):
         off = me * CL + blk * BLK - RIM
+        cols_of = nbr[:, pl.ds(blk * BLK, BLK)].T
         for j in range(NNB):
-            col = nbr[pl.ds(blk * BLK, BLK), j : j + 1] - off
+            col = cols_of[:, j : j + 1] - off
             gone[blk, j] = one_hot(wl == col)
+
+    def gather(q, i):
+        d = i // 2
+        first = ((g + d + 1) % GROUPS) * MEMBERS + (i % 2) * 16
+        parts = [hv[q][jnp.maximum(src[k % 2, first + k // 2], 0)] for k in range(32)]
+        tile = jnp.concatenate(
+            [jnp.concatenate(parts[:16], axis=0), jnp.concatenate(parts[16:], axis=0)], axis=1
+        )
+        turned = dot(perm[...], tile).astype(BF16)
+        for h in range(HC):
+            for s in range(2):
+                arows[
+                    pl.ds(pl.multiple_of(i * 32 + s * 16, 16), 16), pl.ds((q * HC + h) * NB, NB)
+                ] = turned[h * 16 : (h + 1) * 16, s * NB : (s + 1) * NB]
 
     acc = jnp.zeros((ROWS, K), F32)
     for q in range(NQ):
         hist_cp[q].wait()
 
-        def gather(i, carry):
-            d = i // 2
-            first = ((g + d + 1) % GROUPS) * 64 + (i % 2) * 32
-            parts = [hv[q][jnp.maximum(src[first + k], 0)] for k in range(32)]
-            tile = jnp.concatenate(
-                [jnp.concatenate(parts[:16], axis=0), jnp.concatenate(parts[16:], axis=0)], axis=1
-            )
-            turned = dot(perm[...], tile).astype(BF16)
-            for h in range(HC):
-                for s in range(2):
-                    arows[
-                        pl.ds(pl.multiple_of(i * 32 + s * 16, 16), 16), pl.ds((q * HC + h) * NB, NB)
-                    ] = turned[h * 16 : (h + 1) * 16, s * NB : (s + 1) * NB]
+        def gathers(i, carry):
+            for k in range(UNROLL):
+                gather(q, i * UNROLL + k)
             return carry
 
-        lax.fori_loop(0, ROWS // 32, gather, 0)
+        lax.fori_loop(0, ROWS // 32 // UNROLL, gathers, 0)
         proj_cp[q].wait()
         acc = acc + dot(
             arows[:, pl.ds(q * HC * NB, HC * NB)], pv[pl.ds(q * HC * NB, HC * NB), :]
@@ -280,7 +291,8 @@
         reduce_group(i, 0)
     halo(0, 0).start()
     halo(0, 1).start()
-    lax.fori_loop(2, 30, reduce_group, 0)
+    for i in range(2, 30):
+        reduce_group(i, 0)
 
     part1[...] = dot(arows[:, : (H - 1) * NB], pv[NB:, :])
     mone[...] = dot(sone[...].astype(BF16), oone[...]).astype(BF16)
@@ -304,7 +316,9 @@
         near_block(t, 3)
 
     def contributions(t):
-        halves = [trans[s].astype(F32) * inb.at[t].reshape(2, PAIRS, 128)[s].astype(F32) for s in range(2)]
+        rays = inb.at[t].reshape(2, PAIRS, 128)
+        factor = trans.reshape(2, PAIRS, 128)
+        halves = [factor[s].astype(F32) * rays[s].astype(F32) for s in range(2)]
         full = jnp.concatenate(halves, axis=1)
         high = full.astype(BF16)
         low = (full - high.astype(F32)).astype(BF16)
@@ -333,9 +347,7 @@
     send_rays(1)
 
     cur0 = currents(oone[...], base[...])
-    cur[0] = cur0
-    out0 = pltpu.make_async_copy(cur.at[0], out_hbm.at[0], out_sem.at[0])
-    out0.start()
+    out[0] = cur0
     newest = cur0.astype(BF16).astype(F32)
     for j in range(NNB):
         weight = ntime[j : j + 1, 0:1].astype(F32)
@@ -346,15 +358,11 @@
 
     wait_rays(1)
     high, low = contributions(1)
-    cur[1] = currents(oone[...], base[...])
-    out1 = pltpu.make_async_copy(cur.at[1], out_hbm.at[1], out_sem.at[1])
-    out1.start()
+    out[1] = currents(oone[...], base[...])
     for t in range(2):
         halo(t, 0).wait_send()
         halo(t, 1).wait_send()
         pltpu.make_async_copy(outb.at[t], outb.at[t], send_sem.at[t]).wait()
-    out0.wait()
-    out1.wait()
 
 
 def body(
@@ -370,10 +378,9 @@
     recv_observers,
     transfer,
 ):
-    halves = transfer.reshape(PAIRS, 2, 128).swapaxes(0, 1)
     args = (
-        send_sources.reshape(PAIRS),
-        recv_observers.reshape(1, PAIRS),
+        send_sources.reshape(DEVICES, 2).T,
+        recv_observers.reshape(DEVICES, 2).T,
         history,
         near_time,
         near_kernel.reshape(NNB * NB, NB),
@@ -381,12 +388,12 @@
         receive_map,
         self_inverse,
         incident,
-        neighbours,
-        halves,
+        neighbours.T,
+        transfer.reshape(DEVICES, 2, K),
     )
     scratch = [
-        pltpu.SMEM((PAIRS,), jnp.int32),
-        pltpu.VMEM((1, PAIRS), jnp.int32),
+        pltpu.SMEM((2, DEVICES), jnp.int32),
+        pltpu.VMEM((2, DEVICES), jnp.int32),
         *[pltpu.VMEM((CL, HC, NB), BF16) for _ in range(NQ)],
         pltpu.VMEM((NNB, H), BF16),
         pltpu.VMEM((NNB * NB, NB), BF16),
@@ -394,9 +401,8 @@
         pltpu.VMEM((K, NB), BF16),
         pltpu.VMEM((NB, NB), BF16),
         pltpu.VMEM((2, CL, NB), F32),
-        pltpu.VMEM((CL, NNB), jnp.int32),
-        pltpu.VMEM((2, PAIRS, 128), BF16),
-        pltpu.VMEM((2, CL, NB), F32),
+        pltpu.VMEM((NNB, CL), jnp.int32),
+        pltpu.VMEM((2, DEVICES, 2, 128), BF16),
         pltpu.VMEM((ROWS, H * NB), BF16),
         pltpu.VMEM((ROWS, K), F32),
         pltpu.VMEM((256, 256), BF16),
@@ -410,23 +416,22 @@
         pltpu.VMEM((CL, NB), F32),
         pltpu.VMEM((2, 2, ROWS // 2, 2, 128), BF16),
         pltpu.VMEM((2, 2, PAIRS // 2, 2, 128), BF16),
-        pltpu.SemaphoreType.DMA((9,)),
+        pltpu.SemaphoreType.DMA((10,)),
         pltpu.SemaphoreType.DMA((NQ,)),
         pltpu.SemaphoreType.DMA((NQ,)),
         pltpu.SemaphoreType.DMA((2,)),
         pltpu.SemaphoreType.DMA((2,)),
         pltpu.SemaphoreType.DMA((2, 2)),
         pltpu.SemaphoreType.DMA((2, 2)),
-        pltpu.SemaphoreType.DMA((2,)),
     ]
     return pl.pallas_call(
         kernel,
         out_shape=jax.ShapeDtypeStruct((2, CL, NB), F32),
-        in_specs=[pl.BlockSpec(memory_space=pl.ANY)] * len(args),
-        out_specs=pl.BlockSpec(memory_space=pl.ANY),
+        in_specs=[pl.BlockSpec(memory_space=pltpu.HBM)] * len(args),
+        out_specs=pl.BlockSpec(memory_space=pltpu.VMEM),
         scratch_shapes=scratch,
         compiler_params=pltpu.CompilerParams(
-            collective_id=0, has_side_effects=True, vmem_limit_bytes=50 << 20
+            collective_id=0, has_side_effects=True, vmem_limit_bytes=64 << 20
         ),
         cost_estimate=pl.CostEstimate(
             flops=4_000_000_000, bytes_accessed=14 << 20, transcendentals=0

time: 43 us -> 29.1 us (0.68)
  local copies, waits for them, and re-layouts: 8.77 us -> 1.87 us
  Pallas kernels: 33.8 us -> 27.1 us
    pallas_call x1, Pallas kernels: 33.8 us -> 27.1 us  [body(): pl.pallas_call(kernel, out_shape=jax.ShapeDtypeStruct((2, CL, NB), F32),...]
    unnamed x14 -> x1, local copies, waits for them, and re-layouts: 7.48 us -> 1.87 us
    reshape x4 -> x0, local copies, waits for them, and re-layouts: 1.29 us -> none  [the longest x2 1.02 us: body(): halves = transfer.reshape(PAIRS, 2, 128).swapaxes(0, 1)]
where the time goes in v2:
time: 29.1 us; the launch traced here: 29 us
  Pallas kernels  27.1 us (93%)
  local copies, waits for them, and re-layouts  1.87 us (6%)
    pallas_call x1, Pallas kernels, body(): pl.pallas_call(kernel, out_shape=jax.ShapeDtypeStruct((2, CL, NB), F32),...  27.1 us
    unnamed x1, local copies, waits for them, and re-layouts  1.87 us

profile of v2, /device:TPU:1, one launch (start us, length us, event | category | flops | bytes accessed | tf_op | source)
XLA Modules:
  0.0 29.0 jit_solution(16786477983014777333)
XLA Ops:
  0.0 27.1 %shard_map.109 = f32[2,512,128]{2,1,0:T(8,128)} custom-call(s32[2,128]{1,0:T(2,128)} %bitcast.14, s32[2,128]{1,0:T(2,128)} %bitcast.15, bf16[512,64,128]{2,1,0:T(8,128)(2,1)} %hist_hbm.1, bf16[8,64]{1,0:T(8,128)(2,1)} %ntime_hbm.1, bf16[1024,128]{1,0:T(8,128)(2,1)} %bitcast.11, bf16[8192,256]{1,0:T(8,128)(2,1)} %bitcast.10, bf16[256,128]{1,0:T(8,128)(2,1)} %rmap_hbm.1, ...), custom_call_target="tpu_custom_call" | custom-call | flops 4000000000 | bytes 14680064 | tf_op jit(solution)/shard_map/pallas_call | solution.py:427
  27.1 1.9 %copy.13 = f32[2,512,128]{2,1,0:T(8,128)} copy(f32[2,512,128]{2,1,0:T(8,128)} %shard_map.109) | data formatting | bytes 1048576

commit v3 on v2

--- a/solution.py
+++ b/solution.py
@@ -426,17 +426,17 @@
     ]
     return pl.pallas_call(
         kernel,
-        out_shape=jax.ShapeDtypeStruct((2, CL, NB), F32),
+        out_shape=pltpu.VMEM((2, CL, NB), F32),
         in_specs=[pl.BlockSpec(memory_space=pltpu.HBM)] * len(args),
         out_specs=pl.BlockSpec(memory_space=pltpu.VMEM),
         scratch_shapes=scratch,
         compiler_params=pltpu.CompilerParams(
-            collective_id=0, has_side_effects=True, vmem_limit_bytes=64 << 20
+            collective_id=0, has_side_effects=True, vmem_limit_bytes=48 << 20
         ),
         cost_estimate=pl.CostEstimate(
             flops=4_000_000_000, bytes_accessed=14 << 20, transcendentals=0
         ),
-    )(*args)
+    )(*[pltpu.with_memory_space_constraint(a, pltpu.HBM) for a in args])
 
 
 def solution(mesh):

time: 29.1 us -> 27.2 us (0.935)
  local copies, waits for them, and re-layouts: 1.87 us -> 0.8 us
  Pallas kernels: 27.1 us -> 26.3 us
    unnamed x1, local copies, waits for them, and re-layouts: 1.87 us -> 0.8 us
    pallas_call x1, Pallas kernels: 27.1 us -> 26.3 us  [body(): pl.pallas_call(kernel, out_shape=pltpu.VMEM((2, CL, NB), F32), in_specs=[...]
where the time goes in v3:
time: 27.2 us; the launch traced here: 27.1 us
  Pallas kernels  26.3 us (97%)
  local copies, waits for them, and re-layouts  0.8 us (3%)
    pallas_call x1, Pallas kernels, body(): pl.pallas_call(kernel, out_shape=pltpu.VMEM((2, CL, NB), F32), in_specs=[...  26.3 us
    unnamed x1, local copies, waits for them, and re-layouts  0.8 us

profile of v3, /device:TPU:1, one launch (start us, length us, event | category | flops | bytes accessed | tf_op | source)
XLA Modules:
  0.0 27.1 jit_solution(15360639192718725412)
XLA Ops:
  0.0 26.3 %shard_map.109 = f32[2,512,128]{2,1,0:T(8,128)S(1)} custom-call(s32[2,128]{1,0:T(2,128)} %bitcast.14, s32[2,128]{1,0:T(2,128)} %bitcast.15, bf16[512,64,128]{2,1,0:T(8,128)(2,1)} %hist_hbm.1, bf16[8,64]{1,0:T(8,128)(2,1)} %ntime_hbm.1, bf16[1024,128]{1,0:T(8,128)(2,1)} %bitcast.11, bf16[8192,256]{1,0:T(8,128)(2,1)} %bitcast.10, bf16[256,128]{1,0:T(8,128)(2,1)} %rmap_hbm.1, ...), custom_call_target="tpu_custom_call" | custom-call | flops 4000000000 | bytes 14680064 | tf_op jit(solution)/shard_map/pallas_call | solution.py:427
  26.3 0.8 %copy.13 = f32[2,512,128]{2,1,0:T(8,128)} copy(f32[2,512,128]{2,1,0:T(8,128)S(1)} %shard_map.109) | data formatting | bytes 1048576

commit v4 on v3

--- a/solution.py
+++ b/solution.py
@@ -101,13 +101,19 @@
     g = lax.axis_index("group")
     m = lax.axis_index("member")
     me = g * MEMBERS + m
-    z, y, x, c = g, m // 8, (m // 2) % 4, m % 2
+    y, x, c = lax.div(m, 8), lax.rem(lax.div(m, 2), 4), lax.rem(m, 2)
+    at_z = [lax.rem(g + d, 4) for d in range(4)]
+    at_y = [lax.rem(y + d, 4) * 8 for d in range(4)]
+    at_x = [lax.rem(x + d, 4) * 2 for d in range(4)]
+    at_c = [c, 1 - c]
+    at_yx = [[a + b for b in at_x] for a in at_y]
+    at_member = [[[a + b for b in at_c] for a in row] for row in at_yx]
     right = (m + 1) % MEMBERS
     left = (m + MEMBERS - 1) % MEMBERS
 
     def peer(o):
         dz, dy, dx, dc = o
-        return (z + dz) % 4, ((y + dy) % 4) * 8 + ((x + dx) % 4) * 2 + (c + dc) % 2
+        return at_z[dz], at_member[dy][dx][dc]
 
     hv = (hv0, hv1, hv2, hv3)
 
@@ -172,7 +178,8 @@
     by_slot = jnp.concatenate([one_hot(own == seen[s : s + 1]) for s in range(2)], axis=1)
     r = iota((PAIRS, PAIRS), 0)
     weave = one_hot(iota((PAIRS, PAIRS), 1) == (r % DEVICES) * 2 + r // DEVICES)
-    oone[...] = dot(by_slot, weave).astype(BF16)
+    woven = dot(by_slot, weave).astype(BF16)
+    oone[...] = jnp.concatenate([woven, woven], axis=1)
     sub = iota((8, CL), 0)
     lane = iota((8, CL), 1)
 
@@ -322,7 +329,7 @@
         full = jnp.concatenate(halves, axis=1)
         high = full.astype(BF16)
         low = (full - high.astype(F32)).astype(BF16)
-        return high, low
+        return jnp.concatenate([high, low], axis=0)
 
     near_field(0)
     full = base[...]
@@ -331,13 +338,14 @@
     b1 = rest.astype(BF16)
     b2 = (rest - b1.astype(F32)).astype(BF16)
     sel = sone[...].astype(BF16)
-    base_src = dot(sel, b0) + dot(sel, b1) + dot(sel, b2)
+    parts = dot(sel, jnp.concatenate([b0, b1, b2], axis=1))
+    base_src = parts[:, :NB] + parts[:, NB : 2 * NB] + parts[:, 2 * NB :]
 
     wait_rays(0)
-    high, low = contributions(0)
+    terms = contributions(0)
 
     def currents(hot, start):
-        incoming = (dot(hot, high) + dot(hot, low)).astype(BF16)
+        incoming = dot(hot, terms).astype(BF16)
         rhs = (start - dot(incoming, rmap[...])).astype(BF16)
         return dot(rhs, sinv[...])
 
@@ -357,7 +365,7 @@
     near_field(1)
 
     wait_rays(1)
-    high, low = contributions(1)
+    terms = contributions(1)
     out[1] = currents(oone[...], base[...])
     for t in range(2):
         halo(t, 0).wait_send()
@@ -407,9 +415,9 @@
         pltpu.VMEM((ROWS, K), F32),
         pltpu.VMEM((256, 256), BF16),
         pltpu.VMEM((CL // BLK, NNB, BLK, WIN), BF16),
-        pltpu.VMEM((CL, PAIRS), BF16),
+        pltpu.VMEM((CL, 2 * PAIRS), BF16),
         pltpu.VMEM((ROWS, CL), F32),
-        pltpu.VMEM((ROWS, PAIRS), BF16),
+        pltpu.VMEM((ROWS, 2 * PAIRS), BF16),
         pltpu.VMEM((128, 512), BF16),
         pltpu.VMEM((2, NNB, EXT, NB), BF16),
         pltpu.VMEM((NNB, CL, NB), F32),

time: 27.2 us -> 27.1 us (level)
  no operation moved by 1% of the time
where the time goes in v4:
time: 27.1 us; the launch traced here: 27 us
  Pallas kernels  26.2 us (97%)
  local copies, waits for them, and re-layouts  0.8 us (3%)
    pallas_call x1, Pallas kernels, body(): pl.pallas_call(kernel, out_shape=pltpu.VMEM((2, CL, NB), F32), in_specs=[...  26.2 us
    unnamed x1, local copies, waits for them, and re-layouts  0.8 us

profile of v4, /device:TPU:1, one launch (start us, length us, event | category | flops | bytes accessed | tf_op | source)
XLA Modules:
  0.0 27.0 jit_solution(8172809276166166916)
XLA Ops:
  0.0 26.2 %shard_map.109 = f32[2,512,128]{2,1,0:T(8,128)S(1)} custom-call(s32[2,128]{1,0:T(2,128)} %bitcast.14, s32[2,128]{1,0:T(2,128)} %bitcast.15, bf16[512,64,128]{2,1,0:T(8,128)(2,1)} %hist_hbm.1, bf16[8,64]{1,0:T(8,128)(2,1)} %ntime_hbm.1, bf16[1024,128]{1,0:T(8,128)(2,1)} %bitcast.11, bf16[8192,256]{1,0:T(8,128)(2,1)} %bitcast.10, bf16[256,128]{1,0:T(8,128)(2,1)} %rmap_hbm.1, ...), custom_call_target="tpu_custom_call" | custom-call | flops 4000000000 | bytes 14680064 | tf_op jit(solution)/shard_map/pallas_call | solution.py:435
  26.2 0.8 %copy.13 = f32[2,512,128]{2,1,0:T(8,128)} copy(f32[2,512,128]{2,1,0:T(8,128)S(1)} %shard_map.109) | data formatting | bytes 1048576
